TPU v7x, 512 devices: a whole 4x8x8 slice. The times are simulated.
512 devices in a mesh: ens: 2 (over core), lat: 32 (over z, x), chan: 8 (over y).
Axes of the slice: x: 4, y: 8, z: 8, core: 2. Of those that a mesh axis runs over, the one named last changes fastest.
Arguments:
- field: bfloat16 [2, 384, 128, 256], P('ens', 'chan', 'lat'), may hold values from -6 to 6
- cotangent: bfloat16 [2, 384, 128, 256], P('ens', 'chan', 'lat'), may hold values from -6 to 6
- spec_weight: float32 [2, 64, 384], P(None, None, 'chan'), may hold values from -8 to 8
- disco_coef: float32 [128, 9], replicated, may hold values from -2 to 2
- disco_weight: float32 [9, 384], P(None, 'chan'), may hold values from -5 to 5
- disco_rows: int32 [128, 9], replicated, may hold values from 0 to 127, as said below
- disco_shift: int32 [128, 9], replicated, may hold values from -8 to 8
- w_hidden: bfloat16 [384, 768], replicated, may hold values from -0.3125 to 0.3125
- w_output: bfloat16 [768, 384], replicated, may hold values from -0.21875 to 0.21875
Outputs:
- grad_field: bfloat16 [2, 384, 128, 256], P('ens', 'chan', 'lat')
- grad_spec_weight: float32 [2, 64, 384], P(None, None, 'chan')
- grad_disco_weight: float32 [9, 384], P(None, 'chan')
- grad_w_hidden: float32 [384, 768], P('lat')
- grad_w_output: float32 [768, 384], P('lat')
Inputs may be any that keep to these rules, and one draw needn't show every extreme that they name: Entry k of row i of disco_rows names a latitude row within 2 rows of i.
All inputs are finite; a program needn't handle non-finite values.
Results may differ from a plain program's by a relative error of at most 0.013.
Values may be sent and summed in bfloat16 or wider, within the bound.
A program may use at most 64 MiB of HBM per device.

v0:
```python
import math
import jax
import jax.numpy as jnp
from jax import lax
from jax.sharding import PartitionSpec as P

HALO = 2
SHIFT = 8
norm_eps = 1e-06
inv_root_two = 0.7071067811865476
inv_root_tau = 0.3989422804014327
highest = lax.Precision.HIGHEST


def padded_2(block, sides, width):
    for axis, dim in sides:
        count = lax.axis_size(axis)
        forward = [(i, i + 1) for i in range(count - 1)]
        backward = [(target, source) for source, target in forward]
        low = lax.ppermute(
            lax.slice_in_dim(block, block.shape[dim] - width, None, axis=dim), axis, forward
        )
        high = lax.ppermute(lax.slice_in_dim(block, 0, width, axis=dim), axis, backward)
        block = jnp.concatenate([low, block, high], axis=dim)
    return block


def colatitudes(lat_count):
    return (jnp.arange(lat_count, dtype=jnp.int32).astype(jnp.float32) + 0.5) * (
        math.pi / lat_count
    )


def legendre_rows(first_order, order_count, lat_count, degree_count):
    colatitude = colatitudes(lat_count)
    cosine = jnp.cos(colatitude)
    sine_rows = jnp.sin(colatitude)
    orders = (first_order + jnp.arange(order_count, dtype=jnp.int32)).astype(jnp.float32)
    log_start = 0.5 * (
        jnp.log((2.0 * orders + 1.0) / (4.0 * math.pi))
        + lax.lgamma(orders + 0.5)
        - lax.lgamma(orders + 1.0)
        - 0.5 * math.log(math.pi)
    )
    diagonal = jnp.exp(log_start[:, None] + orders[:, None] * jnp.log(sine_rows)[None, :])

    def advance(carry, degree):
        previous, before = carry
        degree_value = degree.astype(jnp.float32)
        above = degree_value > orders
        upper_term = jnp.where(above, 4.0 * degree_value * degree_value - 1.0, 1.0)
        lower_term = jnp.where(above, degree_value * degree_value - orders * orders, 1.0)
        factor = jnp.sqrt(upper_term / lower_term)
        behind = jnp.where(
            above, (degree_value - 1.0) * (degree_value - 1.0) - orders * orders, 0.0
        )
        damping = jnp.sqrt(behind / (4.0 * (degree_value - 1.0) * (degree_value - 1.0) - 1.0))
        recurred = factor[:, None] * (cosine[None, :] * previous - damping[:, None] * before)
        current = jnp.where(
            above[:, None], recurred, jnp.where((degree_value == orders)[:, None], diagonal, 0.0)
        )
        return ((current, previous), current)

    zero_rows = jnp.zeros((order_count, lat_count), jnp.float32)
    finish, stacked = lax.scan(
        advance, (zero_rows, zero_rows), jnp.arange(degree_count, dtype=jnp.int32), unroll=True
    )
    return jnp.transpose(stacked, (1, 0, 2))


def quadrature(lat_count, lon_count):
    return 2.0 * math.pi / lon_count * (math.pi / lat_count) * jnp.sin(colatitudes(lat_count))


def lon_tables(lon_count, mode_count):
    columns = jnp.arange(lon_count, dtype=jnp.int32)
    mode_ids = jnp.arange(mode_count, dtype=jnp.int32)
    phase_ids = columns[:, None] * mode_ids[None, :] % lon_count
    angles = phase_ids.astype(jnp.float32) * (2.0 * math.pi / lon_count)
    cosine = jnp.cos(angles)
    sine_part = jnp.sin(angles)
    forward = jnp.concatenate([cosine, -sine_part], axis=1).astype(jnp.bfloat16)
    doubled = jnp.where(mode_ids == 0, 1.0, 2.0).astype(jnp.float32)[None, :]
    inverse = jnp.transpose(
        jnp.concatenate([doubled * cosine, -doubled * sine_part], axis=1)
    ).astype(jnp.bfloat16)
    return (forward, inverse)


def apply_filter(coeffs, spec_weight):
    real_weight = jnp.transpose(spec_weight[0])[:, None, :]
    imag_weight = jnp.transpose(spec_weight[1])[:, None, :]
    real_part = coeffs[:, 0]
    imag_part = coeffs[:, 1]
    return jnp.stack(
        [
            real_weight * real_part - imag_weight * imag_part,
            real_weight * imag_part + imag_weight * real_part,
        ],
        axis=1,
    )


def filter_adjoint(grads, coeffs, spec_weight):
    real_weight = jnp.transpose(spec_weight[0])[:, None, :]
    imag_weight = jnp.transpose(spec_weight[1])[:, None, :]
    grad_real = grads[:, 0]
    grad_imag = grads[:, 1]
    real_part = coeffs[:, 0]
    imag_part = coeffs[:, 1]
    weight_zero = jnp.transpose(jnp.sum(grad_real * real_part + grad_imag * imag_part, axis=1))
    weight_one = jnp.transpose(jnp.sum(grad_imag * real_part - grad_real * imag_part, axis=1))
    adjoint_coeffs = jnp.stack(
        [
            real_weight * grad_real + imag_weight * grad_imag,
            real_weight * grad_imag - imag_weight * grad_real,
        ],
        axis=1,
    )
    return (adjoint_coeffs, jnp.stack([weight_zero, weight_one], axis=0))


def mlp_backward(mixed_rows, adjoint_rows, w_hidden, w_output):
    mixed32 = mixed_rows.astype(jnp.float32)
    rscale = lax.rsqrt(jnp.mean(mixed32 * mixed32, axis=0, keepdims=True) + norm_eps)
    normed32 = mixed32 * rscale
    normed = normed32.astype(jnp.bfloat16)
    preact = lax.dot_general(
        w_hidden, normed, (((0,), (0,)), ((), ())), preferred_element_type=jnp.float32
    )
    activated = jax.nn.gelu(preact, approximate=False).astype(jnp.bfloat16)
    grad_output = lax.dot_general(
        activated, adjoint_rows, (((1,), (1,)), ((), ())), preferred_element_type=jnp.float32
    )
    grad_act = lax.dot_general(
        w_output, adjoint_rows, (((1,), (0,)), ((), ())), preferred_element_type=jnp.float32
    )
    cumulative = 0.5 * (1.0 + lax.erf(preact * inv_root_two))
    density = jnp.exp(-0.5 * preact * preact) * inv_root_tau
    grad_pre = (grad_act * (cumulative + preact * density)).astype(jnp.bfloat16)
    grad_hidden = lax.dot_general(
        normed, grad_pre, (((1,), (1,)), ((), ())), preferred_element_type=jnp.float32
    )
    grad_normed = lax.dot_general(
        w_hidden, grad_pre, (((1,), (0,)), ((), ())), preferred_element_type=jnp.float32
    )
    grad_mixed = (
        rscale * (grad_normed - normed32 * jnp.mean(grad_normed * normed32, axis=0, keepdims=True))
    ).astype(jnp.bfloat16)
    return (grad_mixed, grad_hidden, grad_output)


def to_modes(spectrum):
    return lax.all_to_all(spectrum, "lat", split_axis=3, concat_axis=1, tiled=True)


def to_bands(spectrum):
    return lax.all_to_all(spectrum, "lat", split_axis=1, concat_axis=3, tiled=True)


def wrap_lon(values, width):
    return jnp.concatenate([values[:, :, -width:], values, values[:, :, :width]], axis=2)


def disco_kernel(rows_tab, shift_tab, coef_tab, centre, disco_weight):
    row_step = rows_tab - centre[:, None] + HALO
    lon_step = shift_tab + SHIFT
    reach = jnp.arange(2 * HALO + 1, dtype=jnp.int32)
    span = jnp.arange(2 * SHIFT + 1, dtype=jnp.int32)
    onehot = (
        (row_step[:, :, None, None] == reach[None, None, :, None])
        & (lon_step[:, :, None, None] == span[None, None, None, :])
    ).astype(jnp.float32)
    kernel = jnp.einsum("rk,rkpq,kc->crpq", coef_tab, onehot, disco_weight, precision=highest)
    return (onehot, kernel)


def shards(
    field,
    cotangent,
    spec_weight,
    disco_coef,
    disco_weight,
    disco_rows,
    disco_shift,
    w_hidden,
    w_output,
):
    member = field[0]
    adjoint_member = cotangent[0]
    channels, lat_rows, lon_count = member.shape
    band_count = lax.axis_size("lat")
    lat_count = lat_rows * band_count
    mode_count = lat_count // 2
    modes_here = mode_count // band_count
    band_index = lax.axis_index("lat")
    first_row = band_index * lat_rows
    forward, inverse = lon_tables(lon_count, mode_count)
    legendre = legendre_rows(band_index * modes_here, modes_here, lat_count, mode_count)
    weighted = legendre * quadrature(lat_count, lon_count)[None, None, :]
    grad_scale = 1.0 / math.sqrt(lax.axis_size("ens") * lat_count * lon_count)
    reach_count = 2 * HALO + 1
    span_count = 2 * SHIFT + 1
    adjoint_rows = lax.all_to_all(adjoint_member, "chan", split_axis=2, concat_axis=0, tiled=True)
    spectrum = jnp.dot(
        member.reshape(channels * lat_rows, lon_count), forward, preferred_element_type=jnp.float32
    )
    spectrum = spectrum.astype(jnp.bfloat16).reshape(channels, lat_rows, 2, mode_count)
    mode_block = to_modes(spectrum)
    coeffs = jnp.einsum(
        "citm,mli->ctml", mode_block.astype(jnp.float32), weighted, precision=highest
    )
    synthesis = jnp.einsum(
        "ctml,mli->citm", apply_filter(coeffs, spec_weight), legendre, precision=highest
    ).astype(jnp.bfloat16)
    band_block = to_bands(synthesis)
    spectral = jnp.dot(
        band_block.reshape(channels * lat_rows, 2 * mode_count),
        inverse,
        preferred_element_type=jnp.float32,
    )
    spectral = spectral.reshape(channels, lat_rows, lon_count)
    global_rows = first_row + jnp.arange(lat_rows, dtype=jnp.int32)
    rows_here = lax.dynamic_slice_in_dim(disco_rows, first_row, lat_rows, 0)
    shift_here = lax.dynamic_slice_in_dim(disco_shift, first_row, lat_rows, 0)
    coef_here = lax.dynamic_slice_in_dim(disco_coef, first_row, lat_rows, 0)
    onehot_here, kernel_here = disco_kernel(
        rows_here, shift_here, coef_here, global_rows, disco_weight
    )
    padded = padded_2(member, (("lat", 1),), HALO)
    wide_field = wrap_lon(padded, SHIFT)
    disco_out = jnp.zeros((channels, lat_rows, lon_count), jnp.float32)
    for reach in range(reach_count):
        for span in range(span_count):
            window = wide_field[:, reach : reach + lat_rows, span : span + lon_count].astype(
                jnp.float32
            )
            disco_out = disco_out + kernel_here[:, :, reach, span][:, :, None] * window
    mixed_field = (spectral + disco_out).astype(jnp.bfloat16)
    mixed_rows = lax.all_to_all(mixed_field, "chan", split_axis=2, concat_axis=0, tiled=True)
    all_channels = mixed_rows.shape[0]
    row_width = mixed_rows.shape[2]
    grad_rows, grad_hidden, grad_output = mlp_backward(
        mixed_rows.reshape(all_channels, lat_rows * row_width),
        adjoint_rows.reshape(all_channels, lat_rows * row_width),
        w_hidden,
        w_output,
    )
    grad_field = lax.all_to_all(
        grad_rows.reshape(all_channels, lat_rows, row_width),
        "chan",
        split_axis=0,
        concat_axis=2,
        tiled=True,
    )
    grad_synth = lax.dot_general(
        grad_field.reshape(channels * lat_rows, lon_count),
        inverse,
        (((1,), (1,)), ((), ())),
        preferred_element_type=jnp.float32,
    )
    grad_synth = grad_synth.astype(jnp.bfloat16).reshape(channels, lat_rows, 2, mode_count)
    grad_modes = to_modes(grad_synth)
    grad_filtered = jnp.einsum(
        "citm,mli->ctml", grad_modes.astype(jnp.float32), legendre, precision=highest
    )
    grad_coeffs, filter_part = filter_adjoint(grad_filtered, coeffs, spec_weight)
    grad_spectrum = jnp.einsum("ctml,mli->citm", grad_coeffs, weighted, precision=highest).astype(
        jnp.bfloat16
    )
    grad_lines = to_bands(grad_spectrum)
    spectral_back = lax.dot_general(
        grad_lines.reshape(channels * lat_rows, 2 * mode_count),
        forward,
        (((1,), (1,)), ((), ())),
        preferred_element_type=jnp.float32,
    )
    spectral_back = spectral_back.reshape(channels, lat_rows, lon_count)
    grad_wide = grad_field.astype(jnp.float32)
    reach_sums = []
    for reach in range(reach_count):
        span_sums = []
        for span in range(span_count):
            window = wide_field[:, reach : reach + lat_rows, span : span + lon_count].astype(
                jnp.float32
            )
            span_sums.append(jnp.sum(window * grad_wide, axis=2))
        reach_sums.append(jnp.stack(span_sums, axis=2))
    inner_sum = jnp.stack(reach_sums, axis=2)
    disco_part = jnp.einsum(
        "ik,ikpq,cipq->kc", coef_here, onehot_here, inner_sum, precision=highest
    )
    rimmed = padded_2(grad_field, (("lat", 1),), HALO)
    wide_grads = wrap_lon(rimmed, SHIFT)
    ext_count = lat_rows + 2 * HALO
    ext_rows = first_row - HALO + jnp.arange(ext_count, dtype=jnp.int32)
    rows_ext = lax.dynamic_slice_in_dim(
        jnp.pad(disco_rows, ((HALO, HALO), (0, 0))), first_row, ext_count, 0
    )
    shift_ext = lax.dynamic_slice_in_dim(
        jnp.pad(disco_shift, ((HALO, HALO), (0, 0))), first_row, ext_count, 0
    )
    coef_ext = lax.dynamic_slice_in_dim(
        jnp.pad(disco_coef, ((HALO, HALO), (0, 0))), first_row, ext_count, 0
    )
    onehot_ext, kernel_ext = disco_kernel(rows_ext, shift_ext, coef_ext, ext_rows, disco_weight)
    spread = jnp.zeros((channels, lat_rows, lon_count), jnp.float32)
    for reach in range(reach_count):
        row_start = 2 * HALO - reach
        for span in range(span_count):
            col_start = 2 * SHIFT - span
            window = wide_grads[
                :, row_start : row_start + lat_rows, col_start : col_start + lon_count
            ].astype(jnp.float32)
            spread = (
                spread
                + kernel_ext[:, row_start : row_start + lat_rows, reach, span][:, :, None] * window
            )
    grad_input = (adjoint_member.astype(jnp.float32) + spectral_back + spread).astype(jnp.bfloat16)
    filter_total, disco_total = lax.psum((filter_part, disco_part), ("ens", "lat"))
    total_hidden, total_output = lax.psum((grad_hidden, grad_output), ("ens", "lat", "chan"))
    hidden_rows = total_hidden.shape[0] // band_count
    output_rows = total_output.shape[0] // band_count
    share_hidden = lax.dynamic_slice_in_dim(total_hidden, band_index * hidden_rows, hidden_rows, 0)
    share_output = lax.dynamic_slice_in_dim(total_output, band_index * output_rows, output_rows, 0)
    return (
        grad_input[None],
        filter_total,
        disco_total * grad_scale,
        share_hidden * grad_scale,
        share_output * grad_scale,
    )


def solution(mesh):
    in_specs = (
        P("ens", "chan", "lat", None),
        P("ens", "chan", "lat", None),
        P(None, None, "chan"),
        P(),
        P(None, "chan"),
        P(),
        P(),
        P(),
        P(),
    )
    out_specs = (
        P("ens", "chan", "lat", None),
        P(None, None, "chan"),
        P(None, "chan"),
        P("lat", None),
        P("lat", None),
    )
    return jax.shard_map(shards, mesh=mesh, in_specs=in_specs, out_specs=out_specs, check_vma=False)
```

profile of v0, /device:TPU:256, one launch (start us, length us, event | category | flops | bytes accessed | tf_op | source)
XLA Modules:
  0.0 485.7 jit_solution(5748793667730272015)
XLA Ops:
  7.5 0.9 reshape_squeeze.3
  8.9 0.8 reshape.55196
  9.7 9.9 %all-to-all-start = ((bf16[32,2,384]{2,1,0:T(2,128)(2,1)}), bf16[32,2,384]{2,1,0:T(2,128)(2,1)S(1)}, u32[]{:S(2)}, u32[]{:S(2)}) async-start(bf16[32,2,384]{2,1,0:T(2,128)(2,1)} %reshape.55196), calls=%async_computation | async-start | bytes 98304 | tf_op jit(solution)/shard_map/all_to_all | solution.py:154
  19.6 3.4 collective-permute-start
  23.0 5.8 %collective-permute-start.1 = (bf16[48,2,256]{2,0,1:T(8,128)(2,1)S(1)}, bf16[48,2,256]{2,0,1:T(8,128)(2,1)S(1)}, u32[]{:S(2)}, u32[]{:S(2)}) collective-permute-start(bf16[48,2,256]{2,0,1:T(8,128)(2,1)S(1)} %get-tuple-element.536), channel_id=1, source_target_pairs={{8,0},{16,8},{24,16},{32,24},{40,32},{48,40},{56,48},{64,56},{72,6... | collective-permute-start | bytes 147464 | tf_op jit(solution)/shard_map/ppermute | solution.py:23
  77.1 0.9 convolution_bitcast_fusion
  85.0 1.0 reshape.55202
  89.2 7.4 %all-to-all-start.1 = ((bf16[32,2,384]{2,1,0:T(2,128)(2,1)}), bf16[32,2,384]{2,1,0:T(2,128)(2,1)S(1)}, u32[]{:S(2)}, u32[]{:S(2)}) async-start(bf16[32,2,384]{2,1,0:T(2,128)(2,1)} %reshape.55198), calls=%async_computation.1 | async-start | bytes 98304 | tf_op jit(solution)/shard_map/all_to_all | solution.py:158
  96.8 4.9 %all-to-all-done.1 = bf16[32,2,384]{2,1,0:T(2,128)(2,1)S(1)} async-done(((bf16[32,2,384]{2,1,0:T(2,128)(2,1)}), bf16[32,2,384]{2,1,0:T(2,128)(2,1)S(1)}, u32[]{:S(2)}, u32[]{:S(2)}) %all-to-all-start.1) | async-done | bytes 49184 | tf_op jit(solution)/shard_map/all_to_all | solution.py:158
  101.7 7.1 %all-to-all-start.3 = ((bf16[8,2,3072]{2,1,0:T(2,128)(2,1)}), bf16[8,2,3072]{2,1,0:T(2,128)(2,1)S(1)}, u32[]{:S(2)}, u32[]{:S(2)}) async-start(bf16[8,2,3072]{2,1,0:T(2,128)(2,1)} %reshape.55202), calls=%async_computation.3 | async-start | bytes 196608 | tf_op jit(solution)/shard_map/all_to_all | solution.py:204
  109.5 6.0 %fusion.2 = bf16[48,4,256]{2,0,1:T(8,128)(2,1)S(1)} fusion(bf16[48,4,128]{0,2,1:T(8,128)(2,1)S(1)} %bitcast.623, bf16[48,4,256]{2,0,1:T(8,128)(2,1)S(1)} %bitcast.596, f32[48,4]{0,1:T(4,128)S(1)} %bitcast.820, f32[48,4]{0,1:T(4,128)S(1)} %bitcast.821, f32[48,4]{0,1:T(4,128)S(1)} %bitcast.822, f32[48,4]{0,1:T(4,128)S(1)} %bitcast.823, ...), kind=kOutput, calls=%fused_computation.173 | convolution fusion | flops 25493504 | bytes 8339200 | tf_op jit(solution)/shard_map/dot_general | solution.py:217
  115.7 1.0 reshape.55200
  116.7 0.8 all-to-all-done.3
  117.6 6.4 %all-to-all-start.2 = ((bf16[8,2,3072]{2,1,0:T(2,128)(2,1)}), bf16[8,2,3072]{2,1,0:T(2,128)(2,1)S(1)}, u32[]{:S(2)}, u32[]{:S(2)}) async-start(bf16[8,2,3072]{2,1,0:T(2,128)(2,1)} %reshape.55200), calls=%async_computation.2 | async-start | bytes 196608 | tf_op jit(solution)/shard_map/all_to_all | solution.py:240
  125.2 7.5 %all-to-all-done.2 = bf16[8,2,3072]{2,1,0:T(2,128)(2,1)S(1)} async-done(((bf16[8,2,3072]{2,1,0:T(2,128)(2,1)}), bf16[8,2,3072]{2,1,0:T(2,128)(2,1)S(1)}, u32[]{:S(2)}, u32[]{:S(2)}) %all-to-all-start.2) | async-done | bytes 98336 | tf_op jit(solution)/shard_map/all_to_all | solution.py:240
  134.6 2.0 fusion.24
  137.8 1.0 reshape.55204
  138.8 3.4 all-to-all-start.4
  142.5 1.5 fusion.613
  144.0 6.9 %all-to-all-done.4 = bf16[8,2,3072]{2,1,0:T(2,128)(2,1)S(1)} async-done(((bf16[8,2,3072]{2,1,0:T(2,128)(2,1)}), bf16[8,2,3072]{2,1,0:T(2,128)(2,1)S(1)}, u32[]{:S(2)}, u32[]{:S(2)}) %all-to-all-start.4) | async-done | bytes 98336 | tf_op jit(solution)/shard_map/all_to_all | solution.py:249
  152.1 1.1 fusion.210
  153.2 1.2 fusion.219
  154.4 1.1 fusion.209
  155.5 1.2 fusion.218
  158.3 8.6 %all-to-all-start.5 = ((bf16[32,2,384]{2,1,0:T(2,128)(2,1)}), bf16[32,2,384]{2,1,0:T(2,128)(2,1)S(1)}, u32[]{:S(2)}, u32[]{:S(2)}) async-start(bf16[32,2,384]{2,1,0:T(2,128)(2,1)} %reshape.55206), calls=%async_computation.5 | async-start | bytes 98304 | tf_op jit(solution)/shard_map/all_to_all | solution.py:154
  166.9 3.4 collective-permute-start.2
  170.3 5.8 %collective-permute-start.3 = (bf16[48,2,256]{2,0,1:T(8,128)(2,1)S(1)}, bf16[48,2,256]{2,0,1:T(8,128)(2,1)S(1)}, u32[]{:S(2)}, u32[]{:S(2)}) collective-permute-start(bf16[48,2,256]{2,0,1:T(8,128)(2,1)S(1)} %get-tuple-element.534), channel_id=1, source_target_pairs={{8,0},{16,8},{24,16},{32,24},{40,32},{48,40},{56,48},{64,56},{72,6... | collective-permute-start | bytes 147464 | tf_op jit(solution)/shard_map/ppermute | solution.py:23
  180.3 10.2 %all-to-all-start.6 = ((bf16[32,2,384]{2,1,0:T(2,128)(2,1)}), bf16[32,2,384]{2,1,0:T(2,128)(2,1)S(1)}, u32[]{:S(2)}, u32[]{:S(2)}) async-start(bf16[32,2,384]{2,1,0:T(2,128)(2,1)} %reshape.55208), calls=%async_computation.6 | async-start | bytes 98304 | tf_op jit(solution)/shard_map/all_to_all | solution.py:158
  190.5 276.9 %all-reduce.4 = (f32[2,64,48]{1,2,0:T(8,128)}, f32[9,48]{1,0:T(8,128)S(1)}) all-reduce(f32[2,64,48]{1,2,0:T(8,128)S(1)} %pad_maximum_fusion.8, f32[9,48]{1,0:T(8,128)S(1)} %convolution_bitcast_fusion.6), channel_id=1, replica_groups=mesh['ens'=2,'lat'=32,'chan'=8] {'ens','lat'}, use_global_device_ids=true, to_apply=%region_5.6 | all-reduce | flops 6576 | bytes 52608 | tf_op jit(solution)/shard_map/psum | solution.py:320
  468.7 6.5 %fusion.4 = bf16[1,48,4,256]{3,1,2,0:T(8,128)(2,1)S(1)} fusion(bf16[48,4,128]{0,2,1:T(8,128)(2,1)S(1)} %bitcast.622, bf16[48,4,256]{2,0,1:T(8,128)(2,1)S(1)} %all_to_all.100, bf16[48,8,256]{2,0,1:T(8,128)(2,1)S(1)} %get-tuple-element.539, bf16[48,8,8]{2,0,1:T(8,128)(2,1)S(1)} %get-tuple-element.520, bf16[48,8,8]{2,0,1:T(8,128)(2,1)S(1)} %get-tuple-element.519, ...), kind=kOutput, calls=%fused_computation.177 | convolution fusion | flops 37191680 | bytes 1076992 | tf_op jit(solution)/shard_map/dot_general | solution.py:272
  475.9 1.5 dynamic-slice_multiply_fusion
  477.5 1.4 dynamic-slice_multiply_fusion.1
  (441 shorter events, 30.0 us)
Async XLA Ops:
  9.7 77.4 %all-to-all-start = ((bf16[32,2,384]{2,1,0:T(2,128)(2,1)}), bf16[32,2,384]{2,1,0:T(2,128)(2,1)S(1)}, u32[]{:S(2)}, u32[]{:S(2)}) async-start(bf16[32,2,384]{2,1,0:T(2,128)(2,1)} %reshape.55196), calls=%async_computation | async-start | bytes 98304 | tf_op jit(solution)/shard_map/all_to_all | solution.py:154
  19.6 67.3 %collective-permute-start = (bf16[48,2,256]{2,0,1:T(8,128)(2,1)S(1)}, bf16[48,2,256]{2,0,1:T(8,128)(2,1)S(1)}, u32[]{:S(2)}, u32[]{:S(2)}) collective-permute-start(bf16[48,2,256]{2,0,1:T(8,128)(2,1)S(1)} %get-tuple-element.537), channel_id=1, source_target_pairs={{0,8},{8,16},{16,24},{24,32},{32,40},{40,48},{48,56},{56,64},{64,7... | collective-permute-start | bytes 147464 | tf_op jit(solution)/shard_map/ppermute | solution.py:20
  23.0 63.9 %collective-permute-start.1 = (bf16[48,2,256]{2,0,1:T(8,128)(2,1)S(1)}, bf16[48,2,256]{2,0,1:T(8,128)(2,1)S(1)}, u32[]{:S(2)}, u32[]{:S(2)}) collective-permute-start(bf16[48,2,256]{2,0,1:T(8,128)(2,1)S(1)} %get-tuple-element.536), channel_id=1, source_target_pairs={{8,0},{16,8},{24,16},{32,24},{40,32},{48,40},{56,48},{64,56},{72,6... | collective-permute-start | bytes 147464 | tf_op jit(solution)/shard_map/ppermute | solution.py:23
  89.2 12.5 %all-to-all-start.1 = ((bf16[32,2,384]{2,1,0:T(2,128)(2,1)}), bf16[32,2,384]{2,1,0:T(2,128)(2,1)S(1)}, u32[]{:S(2)}, u32[]{:S(2)}) async-start(bf16[32,2,384]{2,1,0:T(2,128)(2,1)} %reshape.55198), calls=%async_computation.1 | async-start | bytes 98304 | tf_op jit(solution)/shard_map/all_to_all | solution.py:158
  101.7 15.8 %all-to-all-start.3 = ((bf16[8,2,3072]{2,1,0:T(2,128)(2,1)}), bf16[8,2,3072]{2,1,0:T(2,128)(2,1)S(1)}, u32[]{:S(2)}, u32[]{:S(2)}) async-start(bf16[8,2,3072]{2,1,0:T(2,128)(2,1)} %reshape.55202), calls=%async_computation.3 | async-start | bytes 196608 | tf_op jit(solution)/shard_map/all_to_all | solution.py:204
  117.6 15.1 %all-to-all-start.2 = ((bf16[8,2,3072]{2,1,0:T(2,128)(2,1)}), bf16[8,2,3072]{2,1,0:T(2,128)(2,1)S(1)}, u32[]{:S(2)}, u32[]{:S(2)}) async-start(bf16[8,2,3072]{2,1,0:T(2,128)(2,1)} %reshape.55200), calls=%async_computation.2 | async-start | bytes 196608 | tf_op jit(solution)/shard_map/all_to_all | solution.py:240
  138.8 12.0 %all-to-all-start.4 = ((bf16[8,2,3072]{2,1,0:T(2,128)(2,1)}), bf16[8,2,3072]{2,1,0:T(2,128)(2,1)S(1)}, u32[]{:S(2)}, u32[]{:S(2)}) async-start(bf16[8,2,3072]{2,1,0:T(2,128)(2,1)} %reshape.55204), calls=%async_computation.4 | async-start | bytes 196608 | tf_op jit(solution)/shard_map/all_to_all | solution.py:249
  142.2 333.7 %all-reduce.7.cloned.1.call-start = ((), (), s32[]{:S(2)}) async-start(), calls=%async_computation.7 | async-start | bytes 4718592 | tf_op jit(solution)/shard_map/psum | solution.py:321
  158.3 19.9 %all-to-all-start.5 = ((bf16[32,2,384]{2,1,0:T(2,128)(2,1)}), bf16[32,2,384]{2,1,0:T(2,128)(2,1)S(1)}, u32[]{:S(2)}, u32[]{:S(2)}) async-start(bf16[32,2,384]{2,1,0:T(2,128)(2,1)} %reshape.55206), calls=%async_computation.5 | async-start | bytes 98304 | tf_op jit(solution)/shard_map/all_to_all | solution.py:154
  166.9 11.1 %collective-permute-start.2 = (bf16[48,2,256]{2,0,1:T(8,128)(2,1)S(1)}, bf16[48,2,256]{2,0,1:T(8,128)(2,1)S(1)}, u32[]{:S(2)}, u32[]{:S(2)}) collective-permute-start(bf16[48,2,256]{2,0,1:T(8,128)(2,1)S(1)} %get-tuple-element.535), channel_id=1, source_target_pairs={{0,8},{8,16},{16,24},{24,32},{32,40},{40,48},{48,56},{56,64},{64,7... | collective-permute-start | bytes 147464 | tf_op jit(solution)/shard_map/ppermute | solution.py:20
  170.3 7.8 %collective-permute-start.3 = (bf16[48,2,256]{2,0,1:T(8,128)(2,1)S(1)}, bf16[48,2,256]{2,0,1:T(8,128)(2,1)S(1)}, u32[]{:S(2)}, u32[]{:S(2)}) collective-permute-start(bf16[48,2,256]{2,0,1:T(8,128)(2,1)S(1)} %get-tuple-element.534), channel_id=1, source_target_pairs={{8,0},{16,8},{24,16},{32,24},{40,32},{48,40},{56,48},{64,56},{72,6... | collective-permute-start | bytes 147464 | tf_op jit(solution)/shard_map/ppermute | solution.py:23
  178.8 289.6 %copy-start.7 = (f32[48,4,1,1]{0,3,2,1:T(1,128)S(1)}, f32[48,4,1,1]{0,3,2,1:T(1,128)}, u32[]{:S(2)}) copy-start(f32[48,4,1,1]{0,3,2,1:T(1,128)} %get-tuple-element.400) | copy-start | bytes 2308
  178.8 289.6 %copy-start.8 = (f32[48,4,1,1]{0,3,2,1:T(1,128)S(1)}, f32[48,4,1,1]{0,3,2,1:T(1,128)}, u32[]{:S(2)}) copy-start(f32[48,4,1,1]{0,3,2,1:T(1,128)} %get-tuple-element.401) | copy-start | bytes 2308
  178.8 289.6 %copy-start.9 = (f32[48,4,1,1]{0,3,2,1:T(1,128)S(1)}, f32[48,4,1,1]{0,3,2,1:T(1,128)}, u32[]{:S(2)}) copy-start(f32[48,4,1,1]{0,3,2,1:T(1,128)} %get-tuple-element.402) | copy-start | bytes 2308
  178.8 289.6 %copy-start.10 = (f32[48,4,1,1]{0,3,2,1:T(1,128)S(1)}, f32[48,4,1,1]{0,3,2,1:T(1,128)}, u32[]{:S(2)}) copy-start(f32[48,4,1,1]{0,3,2,1:T(1,128)} %get-tuple-element.403) | copy-start | bytes 2308
  178.8 289.6 %copy-start.11 = (f32[48,4,1,1]{0,3,2,1:T(1,128)S(1)}, f32[48,4,1,1]{0,3,2,1:T(1,128)}, u32[]{:S(2)}) copy-start(f32[48,4,1,1]{0,3,2,1:T(1,128)} %get-tuple-element.404) | copy-start | bytes 2308
  178.8 289.6 %copy-start.12 = (f32[48,4,1,1]{0,3,2,1:T(1,128)S(1)}, f32[48,4,1,1]{0,3,2,1:T(1,128)}, u32[]{:S(2)}) copy-start(f32[48,4,1,1]{0,3,2,1:T(1,128)} %get-tuple-element.405) | copy-start | bytes 2308
  178.8 289.6 %copy-start.13 = (f32[48,4,1,1]{0,3,2,1:T(1,128)S(1)}, f32[48,4,1,1]{0,3,2,1:T(1,128)}, u32[]{:S(2)}) copy-start(f32[48,4,1,1]{0,3,2,1:T(1,128)} %get-tuple-element.406) | copy-start | bytes 2308
  178.8 289.6 %copy-start.14 = (f32[48,4,1,1]{0,3,2,1:T(1,128)S(1)}, f32[48,4,1,1]{0,3,2,1:T(1,128)}, u32[]{:S(2)}) copy-start(f32[48,4,1,1]{0,3,2,1:T(1,128)} %get-tuple-element.407) | copy-start | bytes 2308
  178.9 289.6 %copy-start.15 = (f32[48,4,1,1]{0,3,2,1:T(1,128)S(1)}, f32[48,4,1,1]{0,3,2,1:T(1,128)}, u32[]{:S(2)}) copy-start(f32[48,4,1,1]{0,3,2,1:T(1,128)} %get-tuple-element.408) | copy-start | bytes 2308
  178.9 289.6 %copy-start.16 = (f32[48,4,1,1]{0,3,2,1:T(1,128)S(1)}, f32[48,4,1,1]{0,3,2,1:T(1,128)}, u32[]{:S(2)}) copy-start(f32[48,4,1,1]{0,3,2,1:T(1,128)} %get-tuple-element.409) | copy-start | bytes 2308
  178.9 289.6 %copy-start.17 = (f32[48,4,1,1]{0,3,2,1:T(1,128)S(1)}, f32[48,4,1,1]{0,3,2,1:T(1,128)}, u32[]{:S(2)}) copy-start(f32[48,4,1,1]{0,3,2,1:T(1,128)} %get-tuple-element.410) | copy-start | bytes 2308
  178.9 289.6 %copy-start.18 = (f32[48,4,1,1]{0,3,2,1:T(1,128)S(1)}, f32[48,4,1,1]{0,3,2,1:T(1,128)}, u32[]{:S(2)}) copy-start(f32[48,4,1,1]{0,3,2,1:T(1,128)} %get-tuple-element.411) | copy-start | bytes 2308
  178.9 289.6 %copy-start.19 = (f32[48,4,1,1]{0,3,2,1:T(1,128)S(1)}, f32[48,4,1,1]{0,3,2,1:T(1,128)}, u32[]{:S(2)}) copy-start(f32[48,4,1,1]{0,3,2,1:T(1,128)} %get-tuple-element.412) | copy-start | bytes 2308
  178.9 289.6 %copy-start.20 = (f32[48,4,1,1]{0,3,2,1:T(1,128)S(1)}, f32[48,4,1,1]{0,3,2,1:T(1,128)}, u32[]{:S(2)}) copy-start(f32[48,4,1,1]{0,3,2,1:T(1,128)} %get-tuple-element.413) | copy-start | bytes 2308
  178.9 289.6 %copy-start.21 = (f32[48,4,1,1]{0,3,2,1:T(1,128)S(1)}, f32[48,4,1,1]{0,3,2,1:T(1,128)}, u32[]{:S(2)}) copy-start(f32[48,4,1,1]{0,3,2,1:T(1,128)} %get-tuple-element.414) | copy-start | bytes 2308
  178.9 289.6 %copy-start.22 = (f32[48,4,1,1]{0,3,2,1:T(1,128)S(1)}, f32[48,4,1,1]{0,3,2,1:T(1,128)}, u32[]{:S(2)}) copy-start(f32[48,4,1,1]{0,3,2,1:T(1,128)} %get-tuple-element.415) | copy-start | bytes 2308
  178.9 289.6 %copy-start.23 = (f32[48,4,1,1]{0,3,2,1:T(1,128)S(1)}, f32[48,4,1,1]{0,3,2,1:T(1,128)}, u32[]{:S(2)}) copy-start(f32[48,4,1,1]{0,3,2,1:T(1,128)} %get-tuple-element.416) | copy-start | bytes 2308
  178.9 289.6 %copy-start.24 = (f32[48,4,1,1]{0,3,2,1:T(1,128)S(1)}, f32[48,4,1,1]{0,3,2,1:T(1,128)}, u32[]{:S(2)}) copy-start(f32[48,4,1,1]{0,3,2,1:T(1,128)} %get-tuple-element.417) | copy-start | bytes 2308
  179.0 289.6 %copy-start.25 = (f32[48,4,1,1]{0,3,2,1:T(1,128)S(1)}, f32[48,4,1,1]{0,3,2,1:T(1,128)}, u32[]{:S(2)}) copy-start(f32[48,4,1,1]{0,3,2,1:T(1,128)} %get-tuple-element.418) | copy-start | bytes 2308
  179.0 289.6 %copy-start.26 = (f32[48,4,1,1]{0,3,2,1:T(1,128)S(1)}, f32[48,4,1,1]{0,3,2,1:T(1,128)}, u32[]{:S(2)}) copy-start(f32[48,4,1,1]{0,3,2,1:T(1,128)} %get-tuple-element.419) | copy-start | bytes 2308
  180.3 287.7 %all-to-all-start.6 = ((bf16[32,2,384]{2,1,0:T(2,128)(2,1)}), bf16[32,2,384]{2,1,0:T(2,128)(2,1)S(1)}, u32[]{:S(2)}, u32[]{:S(2)}) async-start(bf16[32,2,384]{2,1,0:T(2,128)(2,1)} %reshape.55208), calls=%async_computation.6 | async-start | bytes 98304 | tf_op jit(solution)/shard_map/all_to_all | solution.py:158
  (63 other events, 5268.2 us)
Sparse Core Ops, SparseCore 0:
  148.1 279.6 all-reduce.6
where the time goes:
time: 487 us; the launch traced here: 486 us
  blocking collectives  277 us (57%)
  starting transfers between devices  71.5 us (15%)
  between operations  58.2 us (12%)
  local copies, waits for them, and re-layouts  24.1 us (5%)
  matrix products  20.6 us (4%)
  waiting for transfers between devices  20.2 us (4%)
  other arithmetic  14.3 us (3%)
    psum x1, blocking collectives, shards(): lax.psum((filter_part, disco_part), ('ens', 'lat'))  277 us
    all_to_all x2, starting transfers between devices, to_modes(): lax.all_to_all(spectrum, 'lat', split_axis=3, concat_axis=1, tiled=True)  18.5 us
    all_to_all x2, starting transfers between devices, to_bands(): lax.all_to_all(spectrum, 'lat', split_axis=1, concat_axis=3, tiled=True)  17.6 us
    ppermute x2, starting transfers between devices, padded_2(): lax.ppermute(lax.slice_in_dim(block, 0, width, axis=dim), axis, backward)  11.6 us
  transfers between devices with their start and end apart: 12, of which 4 were waited for; matrix products, arithmetic and copies ran while one was open for 9% of the time, Pallas kernels for 0%

commit v1 on v0

--- a/solution.py
+++ b/solution.py
@@ -317,7 +317,7 @@
                 + kernel_ext[:, row_start : row_start + lat_rows, reach, span][:, :, None] * window
             )
     grad_input = (adjoint_member.astype(jnp.float32) + spectral_back + spread).astype(jnp.bfloat16)
-    filter_total, disco_total = lax.psum((filter_part, disco_part), ("ens", "lat"))
+    filter_total, disco_total = lax.psum(lax.psum((filter_part, disco_part), "lat"), "ens")
     total_hidden, total_output = lax.psum((grad_hidden, grad_output), ("ens", "lat", "chan"))
     hidden_rows = total_hidden.shape[0] // band_count
     output_rows = total_output.shape[0] // band_count

time: 487 us -> 444 us (0.912)
  the two profiles are of different devices: /device:TPU:256 before, /device:TPU:1 now
where the time goes in v1:
time: 444 us; the launch traced here: 443 us
  blocking collectives  155 us (35%)
  waiting for transfers between devices  105 us (24%)
  starting transfers between devices  65.2 us (15%)
  between operations  58 us (13%)
  local copies, waits for them, and re-layouts  24.1 us (5%)
  matrix products  20.6 us (5%)
  other arithmetic  14.3 us (3%)
    psum x1, blocking collectives, shards(): lax.psum((filter_part, disco_part), 'lat')  115 us
    psum x1, waiting for transfers between devices, shards(): lax.psum((grad_hidden, grad_output), ('ens', 'lat', 'chan'))  82.4 us
    psum x1, blocking collectives, shards(): lax.psum(lax.psum((filter_part, disco_part), 'lat'), 'ens')  40.1 us
    all_to_all x2, starting transfers between devices, to_bands(): lax.all_to_all(spectrum, 'lat', split_axis=1, concat_axis=3, tiled=True)  21.8 us
    all_to_all x2, starting transfers between devices, to_modes(): lax.all_to_all(spectrum, 'lat', split_axis=3, concat_axis=1, tiled=True)  17.6 us
    unnamed x193, local copies, waits for them, and re-layouts  9.26 us
  transfers between devices with their start and end apart: 12, of which 6 were waited for; matrix products, arithmetic and copies ran while one was open for 10% of the time, Pallas kernels for 0%

profile of v1, /device:TPU:1, one launch (start us, length us, event | category | flops | bytes accessed | tf_op | source)
XLA Modules:
  0.0 442.6 jit_solution(16155406760483295653)
XLA Ops:
  7.5 0.9 reshape_squeeze.3
  9.7 13.7 %all-to-all-start = ((bf16[32,2,384]{2,1,0:T(2,128)(2,1)}), bf16[32,2,384]{2,1,0:T(2,128)(2,1)S(1)}, u32[]{:S(2)}, u32[]{:S(2)}) async-start(bf16[32,2,384]{2,1,0:T(2,128)(2,1)} %reshape.55196), calls=%async_computation | async-start | bytes 98304 | tf_op jit(solution)/shard_map/all_to_all | solution.py:154
  23.5 3.1 collective-permute-start
  26.6 1.3 collective-permute-start.1
  84.0 1.0 reshape.55202
  88.2 11.0 %all-to-all-start.1 = ((bf16[32,2,384]{2,1,0:T(2,128)(2,1)}), bf16[32,2,384]{2,1,0:T(2,128)(2,1)S(1)}, u32[]{:S(2)}, u32[]{:S(2)}) async-start(bf16[32,2,384]{2,1,0:T(2,128)(2,1)} %reshape.55198), calls=%async_computation.1 | async-start | bytes 98304 | tf_op jit(solution)/shard_map/all_to_all | solution.py:158
  99.4 8.6 %all-to-all-done.1 = bf16[32,2,384]{2,1,0:T(2,128)(2,1)S(1)} async-done(((bf16[32,2,384]{2,1,0:T(2,128)(2,1)}), bf16[32,2,384]{2,1,0:T(2,128)(2,1)S(1)}, u32[]{:S(2)}, u32[]{:S(2)}) %all-to-all-start.1) | async-done | bytes 49184 | tf_op jit(solution)/shard_map/all_to_all | solution.py:158
  107.9 6.8 %all-to-all-start.3 = ((bf16[8,2,3072]{2,1,0:T(2,128)(2,1)}), bf16[8,2,3072]{2,1,0:T(2,128)(2,1)S(1)}, u32[]{:S(2)}, u32[]{:S(2)}) async-start(bf16[8,2,3072]{2,1,0:T(2,128)(2,1)} %reshape.55202), calls=%async_computation.3 | async-start | bytes 196608 | tf_op jit(solution)/shard_map/all_to_all | solution.py:204
  115.5 5.9 %fusion.2 = bf16[48,4,256]{2,0,1:T(8,128)(2,1)S(1)} fusion(bf16[48,4,128]{0,2,1:T(8,128)(2,1)S(1)} %bitcast.623, bf16[48,4,256]{2,0,1:T(8,128)(2,1)S(1)} %bitcast.596, f32[48,4]{0,1:T(4,128)S(1)} %bitcast.820, f32[48,4]{0,1:T(4,128)S(1)} %bitcast.821, f32[48,4]{0,1:T(4,128)S(1)} %bitcast.822, f32[48,4]{0,1:T(4,128)S(1)} %bitcast.823, ...), kind=kOutput, calls=%fused_computation.173 | convolution fusion | flops 25493504 | bytes 8339200 | tf_op jit(solution)/shard_map/dot_general | solution.py:217
  121.6 1.0 reshape.55200
  122.6 6.6 %all-to-all-start.2 = ((bf16[8,2,3072]{2,1,0:T(2,128)(2,1)}), bf16[8,2,3072]{2,1,0:T(2,128)(2,1)S(1)}, u32[]{:S(2)}, u32[]{:S(2)}) async-start(bf16[8,2,3072]{2,1,0:T(2,128)(2,1)} %reshape.55200), calls=%async_computation.2 | async-start | bytes 196608 | tf_op jit(solution)/shard_map/all_to_all | solution.py:240
  130.6 6.3 %all-to-all-done.2 = bf16[8,2,3072]{2,1,0:T(2,128)(2,1)S(1)} async-done(((bf16[8,2,3072]{2,1,0:T(2,128)(2,1)}), bf16[8,2,3072]{2,1,0:T(2,128)(2,1)S(1)}, u32[]{:S(2)}, u32[]{:S(2)}) %all-to-all-start.2) | async-done | bytes 98336 | tf_op jit(solution)/shard_map/all_to_all | solution.py:240
  138.8 2.0 fusion.24
  142.0 1.0 reshape.55204
  143.0 3.4 all-to-all-start.4
  146.7 1.4 fusion.613
  148.1 5.7 %all-to-all-done.4 = bf16[8,2,3072]{2,1,0:T(2,128)(2,1)S(1)} async-done(((bf16[8,2,3072]{2,1,0:T(2,128)(2,1)}), bf16[8,2,3072]{2,1,0:T(2,128)(2,1)S(1)}, u32[]{:S(2)}, u32[]{:S(2)}) %all-to-all-start.4) | async-done | bytes 98336 | tf_op jit(solution)/shard_map/all_to_all | solution.py:249
  155.1 1.1 fusion.210
  156.2 1.2 fusion.219
  157.5 1.1 fusion.209
  158.6 1.2 fusion.218
  161.3 3.9 all-to-all-start.5
  165.2 3.0 collective-permute-start.2
  168.2 1.3 collective-permute-start.3
  171.5 2.1 collective-permute-done.3
  176.0 10.8 %all-to-all-start.6 = ((bf16[32,2,384]{2,1,0:T(2,128)(2,1)}), bf16[32,2,384]{2,1,0:T(2,128)(2,1)S(1)}, u32[]{:S(2)}, u32[]{:S(2)}) async-start(bf16[32,2,384]{2,1,0:T(2,128)(2,1)} %reshape.55208), calls=%async_computation.6 | async-start | bytes 98304 | tf_op jit(solution)/shard_map/all_to_all | solution.py:158
  186.8 115.1 %all-reduce.4 = (f32[2,64,48]{1,2,0:T(8,128)S(1)}, f32[9,48]{1,0:T(8,128)S(1)}) all-reduce(f32[2,64,48]{1,2,0:T(8,128)S(1)} %pad_maximum_fusion.8, f32[9,48]{1,0:T(8,128)S(1)} %convolution_bitcast_fusion.6), channel_id=1, replica_groups=mesh['ens'=2,'lat'=32,'chan'=8] {'lat'}, use_global_device_ids=true, to_apply=%region_5.6 | all-reduce | flops 6576 | bytes 52608 | tf_op jit(solution)/shard_map/psum | solution.py:320
  301.9 40.1 %all-reduce.5 = (f32[2,64,48]{1,2,0:T(8,128)}, f32[9,48]{1,0:T(8,128)S(1)}) all-reduce(f32[2,64,48]{1,2,0:T(8,128)S(1)} %get-tuple-element.134, f32[9,48]{1,0:T(8,128)S(1)} %get-tuple-element.135), channel_id=1, replica_groups=mesh['ens'=2,'lat'=32,'chan'=8] {'ens'}, use_global_device_ids=true, to_apply=%region_6.7 | all-reduce | flops 6576 | bytes 52608 | tf_op jit(solution)/shard_map/psum | solution.py:320
  343.3 6.5 %fusion.4 = bf16[1,48,4,256]{3,1,2,0:T(8,128)(2,1)S(1)} fusion(bf16[48,4,128]{0,2,1:T(8,128)(2,1)S(1)} %bitcast.622, bf16[48,4,256]{2,0,1:T(8,128)(2,1)S(1)} %all_to_all.100, bf16[48,8,256]{2,0,1:T(8,128)(2,1)S(1)} %get-tuple-element.541, bf16[48,8,8]{2,0,1:T(8,128)(2,1)S(1)} %get-tuple-element.522, bf16[48,8,8]{2,0,1:T(8,128)(2,1)S(1)} %get-tuple-element.521, ...), kind=kOutput, calls=%fused_computation.177 | convolution fusion | flops 37191680 | bytes 1076992 | tf_op jit(solution)/shard_map/dot_general | solution.py:272
  350.5 82.4 %all-reduce.8.cloned.1.call-done = (f32[384,768]{1,0:T(8,128)}, f32[768,384]{1,0:T(8,128)}) async-done(((f32[384,768]{1,0:T(8,128)}, f32[768,384]{1,0:T(8,128)}), (f32[384,768]{1,0:T(8,128)}, f32[768,384]{1,0:T(8,128)})) %all-reduce.8.cloned.1.call-update) | async-done | bytes 2359312 | tf_op jit(solution)/shard_map/psum | solution.py:321
  432.9 1.5 dynamic-slice_multiply_fusion
  434.4 1.4 dynamic-slice_multiply_fusion.1
  (442 shorter events, 31.9 us)
Async XLA Ops:
  9.7 76.3 %all-to-all-start = ((bf16[32,2,384]{2,1,0:T(2,128)(2,1)}), bf16[32,2,384]{2,1,0:T(2,128)(2,1)S(1)}, u32[]{:S(2)}, u32[]{:S(2)}) async-start(bf16[32,2,384]{2,1,0:T(2,128)(2,1)} %reshape.55196), calls=%async_computation | async-start | bytes 98304 | tf_op jit(solution)/shard_map/all_to_all | solution.py:154
  23.5 62.4 %collective-permute-start = (bf16[48,2,256]{2,0,1:T(8,128)(2,1)S(1)}, bf16[48,2,256]{2,0,1:T(8,128)(2,1)S(1)}, u32[]{:S(2)}, u32[]{:S(2)}) collective-permute-start(bf16[48,2,256]{2,0,1:T(8,128)(2,1)S(1)} %get-tuple-element.539), channel_id=1, source_target_pairs={{0,8},{8,16},{16,24},{24,32},{32,40},{40,48},{48,56},{56,64},{64,7... | collective-permute-start | bytes 147464 | tf_op jit(solution)/shard_map/ppermute | solution.py:20
  26.6 59.3 %collective-permute-start.1 = (bf16[48,2,256]{2,0,1:T(8,128)(2,1)S(1)}, bf16[48,2,256]{2,0,1:T(8,128)(2,1)S(1)}, u32[]{:S(2)}, u32[]{:S(2)}) collective-permute-start(bf16[48,2,256]{2,0,1:T(8,128)(2,1)S(1)} %get-tuple-element.538), channel_id=1, source_target_pairs={{8,0},{16,8},{24,16},{32,24},{40,32},{48,40},{56,48},{64,56},{72,6... | collective-permute-start | bytes 147464 | tf_op jit(solution)/shard_map/ppermute | solution.py:23
  88.2 19.7 %all-to-all-start.1 = ((bf16[32,2,384]{2,1,0:T(2,128)(2,1)}), bf16[32,2,384]{2,1,0:T(2,128)(2,1)S(1)}, u32[]{:S(2)}, u32[]{:S(2)}) async-start(bf16[32,2,384]{2,1,0:T(2,128)(2,1)} %reshape.55198), calls=%async_computation.1 | async-start | bytes 98304 | tf_op jit(solution)/shard_map/all_to_all | solution.py:158
  107.9 14.7 %all-to-all-start.3 = ((bf16[8,2,3072]{2,1,0:T(2,128)(2,1)}), bf16[8,2,3072]{2,1,0:T(2,128)(2,1)S(1)}, u32[]{:S(2)}, u32[]{:S(2)}) async-start(bf16[8,2,3072]{2,1,0:T(2,128)(2,1)} %reshape.55202), calls=%async_computation.3 | async-start | bytes 196608 | tf_op jit(solution)/shard_map/all_to_all | solution.py:204
  122.6 14.2 %all-to-all-start.2 = ((bf16[8,2,3072]{2,1,0:T(2,128)(2,1)}), bf16[8,2,3072]{2,1,0:T(2,128)(2,1)S(1)}, u32[]{:S(2)}, u32[]{:S(2)}) async-start(bf16[8,2,3072]{2,1,0:T(2,128)(2,1)} %reshape.55200), calls=%async_computation.2 | async-start | bytes 196608 | tf_op jit(solution)/shard_map/all_to_all | solution.py:240
  143.0 10.9 %all-to-all-start.4 = ((bf16[8,2,3072]{2,1,0:T(2,128)(2,1)}), bf16[8,2,3072]{2,1,0:T(2,128)(2,1)S(1)}, u32[]{:S(2)}, u32[]{:S(2)}) async-start(bf16[8,2,3072]{2,1,0:T(2,128)(2,1)} %reshape.55204), calls=%async_computation.4 | async-start | bytes 196608 | tf_op jit(solution)/shard_map/all_to_all | solution.py:249
  146.4 286.5 %all-reduce.8.cloned.1.call-start = ((), (), s32[]{:S(2)}) async-start(), calls=%async_computation.7 | async-start | bytes 4718592 | tf_op jit(solution)/shard_map/psum | solution.py:321
  161.3 12.6 %all-to-all-start.5 = ((bf16[32,2,384]{2,1,0:T(2,128)(2,1)}), bf16[32,2,384]{2,1,0:T(2,128)(2,1)S(1)}, u32[]{:S(2)}, u32[]{:S(2)}) async-start(bf16[32,2,384]{2,1,0:T(2,128)(2,1)} %reshape.55206), calls=%async_computation.5 | async-start | bytes 98304 | tf_op jit(solution)/shard_map/all_to_all | solution.py:154
  165.2 6.3 %collective-permute-start.2 = (bf16[48,2,256]{2,0,1:T(8,128)(2,1)S(1)}, bf16[48,2,256]{2,0,1:T(8,128)(2,1)S(1)}, u32[]{:S(2)}, u32[]{:S(2)}) collective-permute-start(bf16[48,2,256]{2,0,1:T(8,128)(2,1)S(1)} %get-tuple-element.537), channel_id=1, source_target_pairs={{0,8},{8,16},{16,24},{24,32},{32,40},{40,48},{48,56},{56,64},{64,7... | collective-permute-start | bytes 147464 | tf_op jit(solution)/shard_map/ppermute | solution.py:20
  168.2 5.3 %collective-permute-start.3 = (bf16[48,2,256]{2,0,1:T(8,128)(2,1)S(1)}, bf16[48,2,256]{2,0,1:T(8,128)(2,1)S(1)}, u32[]{:S(2)}, u32[]{:S(2)}) collective-permute-start(bf16[48,2,256]{2,0,1:T(8,128)(2,1)S(1)} %get-tuple-element.536), channel_id=1, source_target_pairs={{8,0},{16,8},{24,16},{32,24},{40,32},{48,40},{56,48},{64,56},{72,6... | collective-permute-start | bytes 147464 | tf_op jit(solution)/shard_map/ppermute | solution.py:23
  174.5 168.5 %copy-start.7 = (f32[48,4,1,1]{0,3,2,1:T(1,128)S(1)}, f32[48,4,1,1]{0,3,2,1:T(1,128)}, u32[]{:S(2)}) copy-start(f32[48,4,1,1]{0,3,2,1:T(1,128)} %get-tuple-element.402) | copy-start | bytes 2308
  174.5 168.5 %copy-start.8 = (f32[48,4,1,1]{0,3,2,1:T(1,128)S(1)}, f32[48,4,1,1]{0,3,2,1:T(1,128)}, u32[]{:S(2)}) copy-start(f32[48,4,1,1]{0,3,2,1:T(1,128)} %get-tuple-element.403) | copy-start | bytes 2308
  174.5 168.5 %copy-start.9 = (f32[48,4,1,1]{0,3,2,1:T(1,128)S(1)}, f32[48,4,1,1]{0,3,2,1:T(1,128)}, u32[]{:S(2)}) copy-start(f32[48,4,1,1]{0,3,2,1:T(1,128)} %get-tuple-element.404) | copy-start | bytes 2308
  174.5 168.5 %copy-start.10 = (f32[48,4,1,1]{0,3,2,1:T(1,128)S(1)}, f32[48,4,1,1]{0,3,2,1:T(1,128)}, u32[]{:S(2)}) copy-start(f32[48,4,1,1]{0,3,2,1:T(1,128)} %get-tuple-element.405) | copy-start | bytes 2308
  174.5 168.5 %copy-start.11 = (f32[48,4,1,1]{0,3,2,1:T(1,128)S(1)}, f32[48,4,1,1]{0,3,2,1:T(1,128)}, u32[]{:S(2)}) copy-start(f32[48,4,1,1]{0,3,2,1:T(1,128)} %get-tuple-element.406) | copy-start | bytes 2308
  174.5 168.5 %copy-start.12 = (f32[48,4,1,1]{0,3,2,1:T(1,128)S(1)}, f32[48,4,1,1]{0,3,2,1:T(1,128)}, u32[]{:S(2)}) copy-start(f32[48,4,1,1]{0,3,2,1:T(1,128)} %get-tuple-element.407) | copy-start | bytes 2308
  174.5 168.5 %copy-start.13 = (f32[48,4,1,1]{0,3,2,1:T(1,128)S(1)}, f32[48,4,1,1]{0,3,2,1:T(1,128)}, u32[]{:S(2)}) copy-start(f32[48,4,1,1]{0,3,2,1:T(1,128)} %get-tuple-element.408) | copy-start | bytes 2308
  174.5 168.5 %copy-start.14 = (f32[48,4,1,1]{0,3,2,1:T(1,128)S(1)}, f32[48,4,1,1]{0,3,2,1:T(1,128)}, u32[]{:S(2)}) copy-start(f32[48,4,1,1]{0,3,2,1:T(1,128)} %get-tuple-element.409) | copy-start | bytes 2308
  174.5 168.5 %copy-start.15 = (f32[48,4,1,1]{0,3,2,1:T(1,128)S(1)}, f32[48,4,1,1]{0,3,2,1:T(1,128)}, u32[]{:S(2)}) copy-start(f32[48,4,1,1]{0,3,2,1:T(1,128)} %get-tuple-element.410) | copy-start | bytes 2308
  174.5 168.5 %copy-start.16 = (f32[48,4,1,1]{0,3,2,1:T(1,128)S(1)}, f32[48,4,1,1]{0,3,2,1:T(1,128)}, u32[]{:S(2)}) copy-start(f32[48,4,1,1]{0,3,2,1:T(1,128)} %get-tuple-element.411) | copy-start | bytes 2308
  174.6 168.5 %copy-start.17 = (f32[48,4,1,1]{0,3,2,1:T(1,128)S(1)}, f32[48,4,1,1]{0,3,2,1:T(1,128)}, u32[]{:S(2)}) copy-start(f32[48,4,1,1]{0,3,2,1:T(1,128)} %get-tuple-element.412) | copy-start | bytes 2308
  174.6 168.5 %copy-start.18 = (f32[48,4,1,1]{0,3,2,1:T(1,128)S(1)}, f32[48,4,1,1]{0,3,2,1:T(1,128)}, u32[]{:S(2)}) copy-start(f32[48,4,1,1]{0,3,2,1:T(1,128)} %get-tuple-element.413) | copy-start | bytes 2308
  174.6 168.5 %copy-start.19 = (f32[48,4,1,1]{0,3,2,1:T(1,128)S(1)}, f32[48,4,1,1]{0,3,2,1:T(1,128)}, u32[]{:S(2)}) copy-start(f32[48,4,1,1]{0,3,2,1:T(1,128)} %get-tuple-element.414) | copy-start | bytes 2308
  174.6 168.5 %copy-start.20 = (f32[48,4,1,1]{0,3,2,1:T(1,128)S(1)}, f32[48,4,1,1]{0,3,2,1:T(1,128)}, u32[]{:S(2)}) copy-start(f32[48,4,1,1]{0,3,2,1:T(1,128)} %get-tuple-element.415) | copy-start | bytes 2308
  174.6 168.5 %copy-start.21 = (f32[48,4,1,1]{0,3,2,1:T(1,128)S(1)}, f32[48,4,1,1]{0,3,2,1:T(1,128)}, u32[]{:S(2)}) copy-start(f32[48,4,1,1]{0,3,2,1:T(1,128)} %get-tuple-element.416) | copy-start | bytes 2308
  174.6 168.5 %copy-start.22 = (f32[48,4,1,1]{0,3,2,1:T(1,128)S(1)}, f32[48,4,1,1]{0,3,2,1:T(1,128)}, u32[]{:S(2)}) copy-start(f32[48,4,1,1]{0,3,2,1:T(1,128)} %get-tuple-element.417) | copy-start | bytes 2308
  174.6 168.5 %copy-start.23 = (f32[48,4,1,1]{0,3,2,1:T(1,128)S(1)}, f32[48,4,1,1]{0,3,2,1:T(1,128)}, u32[]{:S(2)}) copy-start(f32[48,4,1,1]{0,3,2,1:T(1,128)} %get-tuple-element.418) | copy-start | bytes 2308
  174.6 168.5 %copy-start.24 = (f32[48,4,1,1]{0,3,2,1:T(1,128)S(1)}, f32[48,4,1,1]{0,3,2,1:T(1,128)}, u32[]{:S(2)}) copy-start(f32[48,4,1,1]{0,3,2,1:T(1,128)} %get-tuple-element.419) | copy-start | bytes 2308
  174.6 168.5 %copy-start.25 = (f32[48,4,1,1]{0,3,2,1:T(1,128)S(1)}, f32[48,4,1,1]{0,3,2,1:T(1,128)}, u32[]{:S(2)}) copy-start(f32[48,4,1,1]{0,3,2,1:T(1,128)} %get-tuple-element.420) | copy-start | bytes 2308
  174.6 168.5 %copy-start.26 = (f32[48,4,1,1]{0,3,2,1:T(1,128)S(1)}, f32[48,4,1,1]{0,3,2,1:T(1,128)}, u32[]{:S(2)}) copy-start(f32[48,4,1,1]{0,3,2,1:T(1,128)} %get-tuple-element.421) | copy-start | bytes 2308
  176.0 166.6 %all-to-all-start.6 = ((bf16[32,2,384]{2,1,0:T(2,128)(2,1)}), bf16[32,2,384]{2,1,0:T(2,128)(2,1)S(1)}, u32[]{:S(2)}, u32[]{:S(2)}) async-start(bf16[32,2,384]{2,1,0:T(2,128)(2,1)} %reshape.55208), calls=%async_computation.6 | async-start | bytes 98304 | tf_op jit(solution)/shard_map/all_to_all | solution.py:158
  (63 other events, 3843.5 us)
Sparse Core Ops, SparseCore 0:
  152.3 280.4 all-reduce.7
